TPU v7x, 512 devices: a whole 4x8x8 slice. The times are simulated.
512 devices in a mesh: row: 16 (over x_lo, z), col: 32 (over y, x_hi, core).
Axes of the slice: x: 4 (x_hi: 2, x_lo: 2; x = x_hi * 2 + x_lo), y: 8, z: 8, core: 2. Of those that a mesh axis runs over, the one named last changes fastest.
Arguments:
- covariance: float32 [16384, 16384], P('row', 'col')
- rotations: float32 [2, 64, 256, 256], P(None, 'row', 'col')
- pairing: int32 [2, 128], replicated, may hold values from 0 to 127, as said below
Outputs:
- transformed: float32 [16384, 16384], P('row', 'col')
Inputs may be any that keep to these rules, and one draw needn't show every extreme that they name: `pairing`: each row is its own inverse and moves entries by at most one: positions 2k + 1 and 2k + 2 either trade places or stay, and every such pair with 2k + 2 a multiple of 4 trades places.
All inputs are finite; a program needn't handle non-finite values.
Results may differ from a plain program's by a relative error of at most 0.00015.
Values sent between devices are 32-bit elements; how exact they have to be, the bound alone decides.
A program may use at most 64 MiB of HBM per device.

v0:
```python
import jax
import jax.numpy as jnp
from jax import lax
from jax.sharding import PartitionSpec as P

BLOCK = 128
ROUNDS = 2


def from_root(value, axis, source):
    kept = jnp.where(lax.axis_index(axis) == source, value, 0).astype(value.dtype)
    return lax.psum(kept, axis)


def extended(block, sides, width):
    for axis, dim in sides:
        count = lax.axis_size(axis)
        forward = [(i, i + 1) for i in range(count - 1)]
        backward = [(target, source) for source, target in forward]
        low = lax.ppermute(
            lax.slice_in_dim(block, block.shape[dim] - width, None, axis=dim), axis, forward
        )
        high = lax.ppermute(lax.slice_in_dim(block, 0, width, axis=dim), axis, backward)
        block = jnp.concatenate([low, block, high], axis=dim)
    return block


def rotate_rows(tile, row_rot):
    shaped = tile.reshape(row_rot.shape[0], row_rot.shape[1], tile.shape[1])
    out = jnp.einsum("kio,kic->koc", row_rot, shaped, precision=lax.Precision.HIGHEST)
    return out.reshape(tile.shape)


def rotate_cols(tile, col_rot):
    shaped = tile.reshape(tile.shape[0], col_rot.shape[0], col_rot.shape[1])
    out = jnp.einsum("rki,kio->rko", shaped, col_rot, precision=lax.Precision.HIGHEST)
    return out.reshape(tile.shape)


def local_order(order_now, first, count):
    picked = lax.dynamic_slice_in_dim(order_now, first, count, 0)
    return picked - first + 1


def body(covariance, rotations, pairing):
    row_idx = lax.axis_index("row")
    col_idx = lax.axis_index("col")
    tile_rows, tile_cols = covariance.shape
    row_blocks = tile_rows // BLOCK
    col_blocks = tile_cols // BLOCK
    row_pairs = row_blocks // 2
    col_pairs = col_blocks // 2
    row_first = row_idx * row_blocks
    col_first = col_idx * col_blocks
    current = covariance
    for rnd in range(ROUNDS):
        row_rot = lax.all_gather(rotations[rnd], "col", axis=1, tiled=True)
        offset = col_idx * col_pairs % row_pairs
        mine = lax.dynamic_slice_in_dim(row_rot, offset, col_pairs, 0)
        col_rot = from_root(mine, "row", col_idx * col_pairs // row_pairs)
        order_now = pairing[rnd]
        row_sel = local_order(order_now, row_first, row_blocks)
        col_sel = local_order(order_now, col_first, col_blocks)
        both = rotate_cols(rotate_rows(current, row_rot), col_rot)
        widened = extended(both, (("row", 0), ("col", 1)), BLOCK)
        blocks = widened.reshape(row_blocks + 2, BLOCK, col_blocks + 2, BLOCK)
        blocks = jnp.take(blocks, row_sel, axis=0)
        blocks = jnp.take(blocks, col_sel, axis=2)
        current = blocks.reshape(tile_rows, tile_cols)
    return current


def solution(mesh):
    in_specs = (P("row", "col"), P(None, "row", "col", None), P())
    out_specs = P("row", "col")
    return jax.shard_map(body, mesh=mesh, in_specs=in_specs, out_specs=out_specs, check_vma=False)
```

profile of v0, /device:TPU:35, one launch (start us, length us, event | category | flops | bytes accessed | tf_op | source)
XLA Modules:
  0.0 478.0 jit_solution(18085767520492862009)
XLA Ops:
  9.0 86.0 %all-gather.5.cloned.1.call-done = f32[1,4,256,256]{3,1,0,2:T(4,128)} async-done(((f32[1,4,8,256]{3,1,0,2:T(4,128)}), f32[1,4,256,256]{3,1,0,2:T(4,128)}) %all-gather.5.cloned.1.call-update) | async-done | bytes 1048592 | tf_op jit(solution)/shard_map/all_gather | solution.py:57
  97.5 80.8 %all-gather.7.cloned.1.call-done = f32[1,4,256,256]{3,1,0,2:T(4,128)} async-done(((f32[1,4,8,256]{3,1,0,2:T(4,128)}), f32[1,4,256,256]{3,1,0,2:T(4,128)}) %all-gather.7.cloned.1.call-update) | async-done | bytes 1048592 | tf_op jit(solution)/shard_map/all_gather | solution.py:57
  180.7 3.3 fusion.5
  184.0 3.5 reshape_reshape.9
  187.5 126.1 %all-reduce.3.cloned.1.call-done = (f32[2,256,256]{1,2,0:T(8,128)}, f32[2,256,256]{1,2,0:T(8,128)}) async-done(((f32[2,256,256]{1,2,0:T(8,128)}, f32[2,256,256]{1,2,0:T(8,128)}), (f32[2,256,256]{1,2,0:T(8,128)}, f32[2,256,256]{1,2,0:T(8,128)})) %all-reduce.3.cloned.1.call-update) | async-done | bytes 1048592 | tf_op jit(solution)/shard_map/psum | solution.py:12
  313.6 3.7 fusion.2
  317.5 4.5 collective-permute-start.1
  326.0 5.3 %collective-permute-done = f32[128,512]{1,0:T(8,128)S(1)} collective-permute-done((f32[128,512]{1,0:T(8,128)S(1)}, f32[128,512]{1,0:T(8,128)S(1)}, u32[]{:S(2)}, u32[]{:S(2)}) %collective-permute-start) | collective-permute-done | bytes 262176 | tf_op jit(solution)/shard_map/ppermute | solution.py:20
  331.4 15.4 %collective-permute-start.3 = (f32[1280,128]{1,0:T(8,128)S(1)}, f32[1280,128]{1,0:T(8,128)S(1)}, u32[]{:S(2)}, u32[]{:S(2)}) collective-permute-start(f32[1280,128]{1,0:T(8,128)S(1)} %get-tuple-element.20), channel_id=1, source_target_pairs={{1,0},{2,1},{3,2},{4,3},{5,4},{6,5},{7,6},{8,7},{9,8},{10,9},{11,1... | collective-permute-start | bytes 1966088 | tf_op jit(solution)/shard_map/ppermute | solution.py:23
  346.8 3.8 collective-permute-start.2
  350.8 13.0 %collective-permute-done.3 = f32[1280,128]{1,0:T(8,128)S(1)} collective-permute-done((f32[1280,128]{1,0:T(8,128)S(1)}, f32[1280,128]{1,0:T(8,128)S(1)}, u32[]{:S(2)}, u32[]{:S(2)}) %collective-permute-start.3) | collective-permute-done | bytes 655392 | tf_op jit(solution)/shard_map/ppermute | solution.py:23
  363.8 2.3 pad_maximum_fusion
  366.0 5.4 %reshape.54 = f32[10,128,6,128]{3,2,1,0:T(8,128)} reshape(f32[1280,768]{1,0:T(8,128)} %pad_maximum_fusion) | data formatting | bytes 7864320 | tf_op jit(solution)/shard_map/reshape | solution.py:66
  371.5 5.1 %copy.51 = f32[10,128,6,128]{3,1,2,0:T(8,128)} copy(f32[10,128,6,128]{3,2,1,0:T(8,128)} %reshape.54) | data formatting | bytes 7864320 | tf_op jit(solution)/shard_map/reshape | solution.py:66
  376.6 4.5 gather_fusion
  381.1 4.0 broadcast_select_fusion.1
  385.1 2.6 gather_fusion.1
  388.0 2.7 copy.52
  390.7 2.2 reshape_reshape.10
  392.9 4.8 %convolution_bitcast_fusion = f32[4,256,512]{1,2,0:T(8,128)} fusion(f32[4,256,512]{2,1,0:T(8,128)S(1)} %reshape_reshape.10, f32[1,4,256,256]{3,1,0,2:T(4,128)S(1)} %copy-done.4), kind=kOutput, calls=%fused_computation.13 | convolution fusion | flops 1610612736 | bytes 5242880 | tf_op jit(solution)/shard_map/kio,kic->koc/dot_general | solution.py:30
  399.6 2.4 reshape_reshape.11
  402.0 3.5 fusion
  407.8 3.4 collective-permute-start.4
  415.1 7.9 %collective-permute-done.4 = f32[128,512]{1,0:T(8,128)S(1)} collective-permute-done((f32[128,512]{1,0:T(8,128)S(1)}, f32[128,512]{1,0:T(8,128)S(1)}, u32[]{:S(2)}, u32[]{:S(2)}) %collective-permute-start.4) | collective-permute-done | bytes 262176 | tf_op jit(solution)/shard_map/ppermute | solution.py:20
  425.0 5.4 %collective-permute-start.6 = (f32[1280,128]{1,0:T(8,128)S(1)}, f32[1280,128]{1,0:T(8,128)S(1)}, u32[]{:S(2)}, u32[]{:S(2)}) collective-permute-start(f32[1280,128]{1,0:T(8,128)S(1)} %get-tuple-element.17), channel_id=1, source_target_pairs={{0,1},{1,2},{2,3},{3,4},{4,5},{5,6},{6,7},{7,8},{8,9},{9,10},{10,1... | collective-permute-start | bytes 1966088 | tf_op jit(solution)/shard_map/ppermute | solution.py:20
  430.4 13.1 %collective-permute-done.7 = f32[1280,128]{1,0:T(8,128)S(1)} collective-permute-done((f32[1280,128]{1,0:T(8,128)S(1)}, f32[1280,128]{1,0:T(8,128)S(1)}, u32[]{:S(2)}, u32[]{:S(2)}) %collective-permute-start.7) | collective-permute-done | bytes 655392 | tf_op jit(solution)/shard_map/ppermute | solution.py:23
  443.5 2.3 pad_maximum_fusion.1
  445.8 5.4 %reshape.56 = f32[10,128,6,128]{3,2,1,0:T(8,128)} reshape(f32[1280,768]{1,0:T(8,128)} %pad_maximum_fusion.1) | data formatting | bytes 7864320 | tf_op jit(solution)/shard_map/reshape | solution.py:66
  451.2 5.1 %copy.60 = f32[10,128,6,128]{3,1,2,0:T(8,128)} copy(f32[10,128,6,128]{3,2,1,0:T(8,128)} %reshape.56) | data formatting | bytes 7864320 | tf_op jit(solution)/shard_map/reshape | solution.py:66
  456.3 4.5 gather_fusion.2
  460.8 4.0 broadcast_select_fusion
  464.9 2.6 gather_fusion.3
  (57 shorter events, 26.1 us)
Async XLA Ops:
  6.5 174.2 %copy-start = (f32[1024,512]{1,0:T(8,128)S(1)}, f32[1024,512]{1,0:T(8,128)}, u32[]{:S(2)}) copy-start(f32[1024,512]{1,0:T(8,128)} %param.7) | copy-start | bytes 6291460
  6.5 88.4 %all-gather.5.cloned.1.call-start = ((), (), s32[]{:S(2)}) async-start(), calls=%async_computation | async-start | bytes 1081344 | tf_op jit(solution)/shard_map/all_gather | solution.py:57
  8.1 170.1 %all-gather.7.cloned.1.call-start = ((), (), s32[]{:S(2)}) async-start(), calls=%async_computation.1 | async-start | bytes 1081344 | tf_op jit(solution)/shard_map/all_gather | solution.py:57
  8.9 304.7 %all-reduce.3.cloned.1.call-start = ((), (), s32[]{:S(2)}) async-start(), calls=%async_computation.2 | async-start | bytes 2097152 | tf_op jit(solution)/shard_map/psum | solution.py:12
  317.3 6.7 %copy-start.2 = (f32[2,256,1024]{2,1,0:T(8,128)}, f32[2,256,1024]{2,1,0:T(8,128)S(1)}, u32[]{:S(2)}) copy-start(f32[2,256,1024]{2,1,0:T(8,128)S(1)} %fusion.2) | copy-start | bytes 6291460
  317.5 8.5 %collective-permute-start.1 = (f32[128,512]{1,0:T(8,128)S(1)}, f32[128,512]{1,0:T(8,128)S(1)}, u32[]{:S(2)}, u32[]{:S(2)}) collective-permute-start(f32[128,512]{1,0:T(8,128)S(1)} %copy.49), channel_id=1, source_target_pairs={{32,0},{64,32},{96,64},{128,96},{160,128},{192,160},{224,192},{256... | collective-permute-start | bytes 786440 | tf_op jit(solution)/shard_map/ppermute | solution.py:23
  322.1 9.2 %collective-permute-start = (f32[128,512]{1,0:T(8,128)S(1)}, f32[128,512]{1,0:T(8,128)S(1)}, u32[]{:S(2)}, u32[]{:S(2)}) collective-permute-start(f32[128,512]{1,0:T(8,128)S(1)} %copy.48), channel_id=1, source_target_pairs={{0,32},{32,64},{64,96},{96,128},{128,160},{160,192},{192,224},{224... | collective-permute-start | bytes 786440 | tf_op jit(solution)/shard_map/ppermute | solution.py:20
  326.0 24.6 %copy-start.6 = (s32[2,128]{1,0:T(2,128)S(1)}, s32[2,128]{1,0:T(2,128)}, u32[]{:S(2)}) copy-start(s32[2,128]{1,0:T(2,128)} %param.9) | copy-start | bytes 3076
  331.4 32.3 %collective-permute-start.3 = (f32[1280,128]{1,0:T(8,128)S(1)}, f32[1280,128]{1,0:T(8,128)S(1)}, u32[]{:S(2)}, u32[]{:S(2)}) collective-permute-start(f32[1280,128]{1,0:T(8,128)S(1)} %get-tuple-element.20), channel_id=1, source_target_pairs={{1,0},{2,1},{3,2},{4,3},{5,4},{6,5},{7,6},{8,7},{9,8},{10,9},{11,1... | collective-permute-start | bytes 1966088 | tf_op jit(solution)/shard_map/ppermute | solution.py:23
  346.8 16.9 %collective-permute-start.2 = (f32[1280,128]{1,0:T(8,128)S(1)}, f32[1280,128]{1,0:T(8,128)S(1)}, u32[]{:S(2)}, u32[]{:S(2)}) collective-permute-start(f32[1280,128]{1,0:T(8,128)S(1)} %get-tuple-element.19), channel_id=1, source_target_pairs={{0,1},{1,2},{2,3},{3,4},{4,5},{5,6},{6,7},{7,8},{8,9},{9,10},{10,1... | collective-permute-start | bytes 1966088 | tf_op jit(solution)/shard_map/ppermute | solution.py:20
  390.7 2.2 copy-start.4
  399.6 2.4 copy-start.5
  405.5 5.6 %copy-start.3 = (f32[2,256,1024]{2,1,0:T(8,128)}, f32[2,256,1024]{2,1,0:T(8,128)S(1)}, u32[]{:S(2)}) copy-start(f32[2,256,1024]{2,1,0:T(8,128)S(1)} %fusion) | copy-start | bytes 6291460
  405.7 9.4 %collective-permute-start.5 = (f32[128,512]{1,0:T(8,128)S(1)}, f32[128,512]{1,0:T(8,128)S(1)}, u32[]{:S(2)}, u32[]{:S(2)}) collective-permute-start(f32[128,512]{1,0:T(8,128)S(1)} %copy.58), channel_id=1, source_target_pairs={{32,0},{64,32},{96,64},{128,96},{160,128},{192,160},{224,192},{256... | collective-permute-start | bytes 786440 | tf_op jit(solution)/shard_map/ppermute | solution.py:23
  407.8 15.2 %collective-permute-start.4 = (f32[128,512]{1,0:T(8,128)S(1)}, f32[128,512]{1,0:T(8,128)S(1)}, u32[]{:S(2)}, u32[]{:S(2)}) collective-permute-start(f32[128,512]{1,0:T(8,128)S(1)} %copy.57), channel_id=1, source_target_pairs={{0,32},{32,64},{64,96},{96,128},{128,160},{160,192},{192,224},{224... | collective-permute-start | bytes 786440 | tf_op jit(solution)/shard_map/ppermute | solution.py:20
  423.1 20.4 %collective-permute-start.7 = (f32[1280,128]{1,0:T(8,128)S(1)}, f32[1280,128]{1,0:T(8,128)S(1)}, u32[]{:S(2)}, u32[]{:S(2)}) collective-permute-start(f32[1280,128]{1,0:T(8,128)S(1)} %get-tuple-element.18), channel_id=1, source_target_pairs={{1,0},{2,1},{3,2},{4,3},{5,4},{6,5},{7,6},{8,7},{9,8},{10,9},{11,1... | collective-permute-start | bytes 1966088 | tf_op jit(solution)/shard_map/ppermute | solution.py:23
  425.0 18.5 %collective-permute-start.6 = (f32[1280,128]{1,0:T(8,128)S(1)}, f32[1280,128]{1,0:T(8,128)S(1)}, u32[]{:S(2)}, u32[]{:S(2)}) collective-permute-start(f32[1280,128]{1,0:T(8,128)S(1)} %get-tuple-element.17), channel_id=1, source_target_pairs={{0,1},{1,2},{2,3},{3,4},{4,5},{5,6},{6,7},{7,8},{8,9},{9,10},{10,1... | collective-permute-start | bytes 1966088 | tf_op jit(solution)/shard_map/ppermute | solution.py:20
  469.1 2.4 copy-start.1
Sparse Core Ops, SparseCore 0:
  10.7 84.1 all-gather.4
  98.3 79.9 all-gather.6
  181.2 132.3 all-reduce.2
where the time goes:
time: 479 us; the launch traced here: 478 us
  waiting for transfers between devices  334 us (70%)
  local copies, waits for them, and re-layouts  61.4 us (13%)
  starting transfers between devices  38.2 us (8%)
  matrix products  15.3 us (3%)
  other arithmetic  15.2 us (3%)
  between operations  13.5 us (3%)
    all_gather x2, waiting for transfers between devices, body(): row_rot = lax.all_gather(rotations[rnd], 'col', axis=1, tiled=True)  167 us
    psum x1, waiting for transfers between devices, from_root(): return lax.psum(kept, axis)  126 us
    ppermute x4, waiting for transfers between devices, extended(): lax.ppermute(lax.slice_in_dim(block, 0, width, axis=dim), axis, backward)  28.1 us
    ppermute x4, starting transfers between devices, extended(): lax.ppermute(lax.slice_in_dim(block, 0, width, axis=dim), axis, backward)  23.7 us
    reshape x4, local copies, waits for them, and re-layouts, body(): blocks = widened.reshape(row_blocks + 2, BLOCK, col_blocks + 2, BLOCK)  21.1 us
    ppermute x4, starting transfers between devices, extended(): lax.ppermute(lax.slice_in_dim(block, block.shape[dim] - width, None, axis...  14.4 us
    ppermute x4, waiting for transfers between devices, extended(): lax.ppermute(lax.slice_in_dim(block, block.shape[dim] - width, None, axis...  13.3 us
  transfers between devices with their start and end apart: 11, of which 8 were waited for; matrix products, arithmetic and copies ran while one was open for 3% of the time, Pallas kernels for 0%

commit v1 on v0

v1 whole, which is shorter than its diff:
```python
import jax
import jax.numpy as jnp
from jax import lax
from jax.experimental import pallas as pl
from jax.experimental.pallas import tpu as pltpu
from jax.sharding import PartitionSpec as P

BLOCK = 128
PAIR = 2 * BLOCK
ROWS, COLS = 16, 32
XL, Z, Y, XH, CORE = 2, 8, 8, 2, 2
RB, CB = 8, 4
RP = RB // 2
MESH = pl.DeviceIdType.MESH
F32, B16 = jnp.float32, jnp.bfloat16


def split(value):
    high = value.astype(B16)
    low = (value - high.astype(F32)).astype(B16)
    return high, low


def dot(a, b):
    return jnp.dot(a, b, preferred_element_type=F32)


def dot3(a, b):
    return dot(a[0], b[0]) + (dot(a[0], b[1]) + dot(a[1], b[0]))


def kernel(
    cov_ref, rot_ref, pair_ref, out_ref,
    cbuf, rr, rc, rrt, rcs, xs, xr, wmid, v, vr, u, ur, ts, tr, tmid, obuf,
    loc_sem, tr_s, tr_r, xl_s, xl_r, xh_s, xh_r, z_s, z_r, y_s, y_r, mt_s, mt_r,
    cx_s, cx_r, vx_s, vx_r, ux_s, ux_r, tx_s, tx_r, out_sem,
):
    r = lax.axis_index("row")
    c = lax.axis_index("col")
    xl, z = r // Z, r % Z
    y, xh, core = c // 4, (c // 2) % 2, c % 2

    def dev(row, col):
        return (row, col)

    mate = dev(r, y * 4 + xh * 2 + (1 - core))
    xh_mate = dev(r, y * 4 + (1 - xh) * 2 + core)
    y_next = dev(r, ((y + 1) % Y) * 4 + xh * 2 + core)
    y_prev = dev(r, ((y + Y - 1) % Y) * 4 + xh * 2 + core)
    xl_mate = dev((1 - xl) * Z + z, c)
    z_next = dev(xl * Z + (z + 1) % Z, c)
    z_prev = dev(xl * Z + (z + Z - 1) % Z, c)
    up = dev((r + ROWS - 1) % ROWS, c)
    down = dev((r + 1) % ROWS, c)
    left = dev(r, (c + COLS - 1) % COLS)
    right = dev(r, (c + 1) % COLS)
    across = [dev(c // 2, 2 * r + h) for h in range(2)]
    stays = [jnp.logical_and(c // 2 == r, core == h) for h in range(2)]
    has_up, has_down = r > 0, r < ROWS - 1
    has_left, has_right = c > 0, c < COLS - 1

    def remote(src, dst, send, recv, device):
        return pltpu.make_async_remote_copy(
            src_ref=src, dst_ref=dst, send_sem=send, recv_sem=recv,
            device_id=device, device_id_type=MESH,
        )

    started = []

    def go(copy):
        copy.start()
        started.append(copy)

    load = pltpu.make_async_copy(cov_ref, cbuf, loc_sem.at[0])
    load.start()
    own = [
        pltpu.make_async_copy(rot_ref.at[t], rr.at[t, :, y, xh, core], loc_sem.at[1 + t])
        for t in range(2)
    ]
    for t in range(2):
        own[t].start()

    barrier = pltpu.get_barrier_semaphore()
    peers = [mate, xh_mate, y_next, y_prev, xl_mate, z_next, z_prev, up, down, left, right]
    for peer in peers:
        pl.semaphore_signal(barrier, inc=1, device_id=peer, device_id_type=MESH)
    for h in range(2):
        @pl.when(jnp.logical_not(stays[h]))
        def _():
            pl.semaphore_signal(barrier, inc=1, device_id=across[h], device_id_type=MESH)
    pl.semaphore_wait(barrier, len(peers) + jnp.where(c // 2 == r, 1, 2))

    row_from = c // 2
    for t in range(2):
        for h in range(2):
            src = rot_ref.at[t, pl.ds(2 * h, 2)]
            dst = rc.at[t, :, row_from // Z, row_from % Z, core]
            there = remote(src, dst, tr_s.at[t, h], tr_r.at[t, core], across[h])
            here = pltpu.make_async_copy(src, dst, tr_r.at[t, core])

            @pl.when(stays[h])
            def _():
                here.start()

            @pl.when(jnp.logical_not(stays[h]))
            def _():
                there.start()

        go(remote(
            rot_ref.at[t], rr.at[t, :, y, xh, core], xh_s.at[t], xh_r.at[t], xh_mate
        ))

    def z_block(t, origin, part=None):
        if part is None:
            return rc.at[t, :, :, origin]
        return rc.at[t, :, part, origin]

    def y_block(t, origin, part=None):
        if part is None:
            return rr.at[t, :, origin, :, core]
        return rr.at[t, :, origin, part, core]

    rings = {
        "z": (z_block, z, Z, z_s, z_r, z_next, z_prev),
        "y": (y_block, y, Y, y_s, y_r, y_next, y_prev),
    }

    def ring_send(name, t, s):
        block, me, n, send, recv, nxt, prv = rings[name]
        last = s == n // 2
        for way, (step, device) in enumerate(((-1, nxt), (1, prv))):
            origin = (me + step * (s - 1) + n) % n
            ref = block(t, origin, way if last else None)
            go(remote(ref, ref, send.at[t, way, s - 1], recv.at[t, way, s - 1], device))

    def ring_wait(name, t, s):
        block, me, n, send, recv, nxt, prv = rings[name]
        last = s == n // 2
        for way, (step, device) in enumerate(((-1, nxt), (1, prv))):
            origin = (me + step * s + n) % n
            ref = block(t, origin, way if last else None)
            remote(
                ref, ref, send.at[t, way, s - 1], recv.at[t, way, s - 1], device
            ).wait_recv()

    def mate_copy(t, origin):
        ref = rr.at[t, :, origin, :, core]
        return remote(ref, ref, mt_s.at[t, origin], mt_r.at[t, origin], mate)

    def mate_wait(t):
        for origin in range(Y):
            ref = rr.at[t, :, origin, :, 1 - core]
            remote(ref, ref, mt_s.at[t, origin], mt_r.at[t, origin], mate).wait_recv()

    def ring_begin(t):
        for s in range(2):
            ref = rc.at[t, :, xl, z, s]
            remote(ref, ref, tr_s.at[t, s], tr_r.at[t, s], mate).wait_recv()
        ref = rc.at[t, :, xl, z]
        go(remote(ref, ref, xl_s.at[t], xl_r.at[t], xl_mate))
        own[t].wait()
        ref = rr.at[t, :, y, 1 - xh, core]
        remote(ref, ref, xh_s.at[t], xh_r.at[t], xh_mate).wait_recv()
        ring_send("y", t, 1)
        go(mate_copy(t, y))
        ref = rc.at[t, :, 1 - xl, z]
        remote(ref, ref, xl_s.at[t], xl_r.at[t], xl_mate).wait_recv()
        ring_send("z", t, 1)

    def ring_steps(t):
        for s in range(1, 5):
            ring_wait("z", t, s)
            if s < 4:
                ring_send("z", t, s + 1)
            ring_wait("y", t, s)
            if s < 4:
                ring_send("y", t, s + 1)
                go(mate_copy(t, (y + Y - s) % Y))
            go(mate_copy(t, (y + s) % Y))
        mate_wait(t)

    def split_cols(t):
        for k in range(2):
            high, low = split(rc[t, k].reshape(PAIR, PAIR))
            rcs[t, k, 0] = high
            rcs[t, k, 1] = low

    def split_rows(t):
        def one(k, _):
            high, low = split(rr[t, k].reshape(PAIR, PAIR).T)
            rrt[t, k, 0] = high
            rrt[t, k, 1] = low
            return 0
        lax.fori_loop(0, RP, one, 0)

    def col_flag(t):
        return pair_ref[t, c * CB + 1] - (c * CB + 1)

    def row_flag(t, which):
        first = r * RB + 1 + 4 * which
        return pair_ref[t, first] - first

    def pick(flag, stay, other):
        return jnp.where(jnp.full(stay.shape, flag, jnp.int32) != 0, other, stay)

    ring_begin(0)
    ring_steps(0)
    load.wait()
    ring_begin(1)

    split_cols(0)
    flag = col_flag(0)
    x_copies = {}
    for k in (0, 3, 1, 2):
        rows = pl.ds(k * PAIR, PAIR)
        one = dot3(split(cbuf[rows, :PAIR]), (rcs[0, 0, 0], rcs[0, 0, 1]))
        xs[k, 0] = one[:, :BLOCK]
        two = dot3(split(cbuf[rows, PAIR:]), (rcs[0, 1, 0], rcs[0, 1, 1]))
        xs[k, 1] = two[:, BLOCK:]
        to_left = remote(xs.at[k, 0], xr.at[k, 1], cx_s.at[k, 0], cx_r.at[k, 1], left)
        to_right = remote(xs.at[k, 1], xr.at[k, 0], cx_s.at[k, 1], cx_r.at[k, 0], right)
        x_copies[k] = (to_left, to_right)

        @pl.when(has_left)
        def _():
            to_left.start()

        @pl.when(has_right)
        def _():
            to_right.start()

        b1, b2 = one[:, BLOCK:], two[:, :BLOCK]
        wmid[rows, :BLOCK] = pick(flag, b1, b2)
        wmid[rows, BLOCK:] = pick(flag, b2, b1)

    split_rows(0)
    vx = {}

    def exchange_rows(buf, got, send, recv, half, which, table):
        edge, device, has = ((0, up, has_up), (RB - 1, down, has_down))[which]
        copy = remote(
            buf.at[half, edge], got.at[half, 1 - which],
            send.at[half, which], recv.at[half, 1 - which], device,
        )
        table[half, which] = (copy, has)

        @pl.when(has)
        def _():
            copy.start()

    def await_rows(buf, got, send, recv, half, which):
        edge, device, has = ((0, up, has_up), (RB - 1, down, has_down))[which]
        copy = remote(
            buf.at[half, edge], got.at[half, which],
            send.at[half, which], recv.at[half, which], device,
        )

        @pl.when(has)
        def _():
            copy.wait_recv()

        @pl.when(jnp.logical_not(has))
        def _():
            got[half, which] = buf[half, edge]

    def mix_rows(t, k, value, buf, half):
        out = dot3((rrt[t, k, 0], rrt[t, k, 1]), split(value))
        buf[half, 2 * k] = out[:BLOCK]
        buf[half, 2 * k + 1] = out[BLOCK:]

    for k in (0, 3, 1, 2):
        mix_rows(0, k, wmid[pl.ds(k * PAIR, PAIR), :], v, 0)
        if k == 0:
            exchange_rows(v, vr, vx_s, vx_r, 0, 0, vx)
        if k == 3:
            exchange_rows(v, vr, vx_s, vx_r, 0, 1, vx)

    ring_steps(1)
    split_rows(1)
    split_cols(1)

    flags = [row_flag(0, 0), row_flag(0, 1)]

    def second_rows(half, k):
        if k == 0:
            pair = (vr[half, 0], pick(flags[0], v[half, 1], v[half, 2]))
        elif k == 1:
            pair = (pick(flags[0], v[half, 2], v[half, 1]), v[half, 4])
        elif k == 2:
            pair = (v[half, 3], pick(flags[1], v[half, 5], v[half, 6]))
        else:
            pair = (pick(flags[1], v[half, 6], v[half, 5]), vr[half, 1])
        mix_rows(1, k, jnp.concatenate(pair, axis=0), u, half)

    ux = {}

    def outer_rows(half):
        for which, k in ((0, 0), (1, 3)):
            await_rows(v, vr, vx_s, vx_r, half, which)
            second_rows(half, k)
            exchange_rows(u, ur, ux_s, ux_r, half, which, ux)

    second_rows(0, 1)
    second_rows(0, 2)
    outer_rows(0)

    def await_side(k, side, own_buf, got, send, recv):
        device, has = ((left, has_left), (right, has_right))[side]
        copy = remote(own_buf.at[k, side], got.at[k, side], send.at[k, side], recv.at[k, side], device)

        @pl.when(has)
        def _():
            copy.wait_recv()

        @pl.when(jnp.logical_not(has))
        def _():
            got[k, side] = own_buf[k, side]

    for k in (0, 3, 1, 2):
        for side in range(2):
            await_side(k, side, xs, xr, cx_s, cx_r)
        mix_rows(0, k, jnp.concatenate((xr[k, 0], xr[k, 1]), axis=1), v, 1)
        if k == 0:
            exchange_rows(v, vr, vx_s, vx_r, 1, 0, vx)
        if k == 3:
            exchange_rows(v, vr, vx_s, vx_r, 1, 1, vx)

    second_rows(1, 1)
    second_rows(1, 2)

    t_copies = {}
    flag2 = col_flag(1)

    def second_cols(g, refs):
        mid = jnp.concatenate([buf[0, i] for buf, i in refs], axis=0)
        edge = jnp.concatenate([buf[1, i] for buf, i in refs], axis=0)
        one = dot3(
            split(jnp.concatenate((edge[:, :BLOCK], mid[:, :BLOCK]), axis=1)),
            (rcs[1, 0, 0], rcs[1, 0, 1]),
        )
        ts[g, 0] = one[:, :BLOCK]
        two = dot3(
            split(jnp.concatenate((mid[:, BLOCK:], edge[:, BLOCK:]), axis=1)),
            (rcs[1, 1, 0], rcs[1, 1, 1]),
        )
        ts[g, 1] = two[:, BLOCK:]
        to_left = remote(ts.at[g, 0], tr.at[g, 1], tx_s.at[g, 0], tx_r.at[g, 1], left)
        to_right = remote(ts.at[g, 1], tr.at[g, 0], tx_s.at[g, 1], tx_r.at[g, 0], right)
        t_copies[g] = (to_left, to_right)

        @pl.when(has_left)
        def _():
            to_left.start()

        @pl.when(has_right)
        def _():
            to_right.start()

        b1, b2 = one[:, BLOCK:], two[:, :BLOCK]
        tmid[g, :, :BLOCK] = pick(flag2, b1, b2)
        tmid[g, :, BLOCK:] = pick(flag2, b2, b1)

    second_cols(0, ((u, 2), (u, 3)))
    second_cols(1, ((u, 4), (u, 5)))
    outer_rows(1)
    second_cols(2, ((u, 1), (u, 6)))
    for half in range(2):
        for which in range(2):
            await_rows(u, ur, ux_s, ux_r, half, which)
    second_cols(3, ((ur, 0), (ur, 1)))

    places = {1: (2, 0), 2: (0, 0), 3: (0, 1), 4: (1, 0), 5: (1, 1), 6: (2, 1), 0: (3, 0), 7: (3, 1)}
    finals = [row_flag(1, 0), row_flag(1, 1)]

    def parts(block):
        g, half = places[block]
        rows = pl.ds(half * BLOCK, BLOCK)
        return tr[g, 0, rows], tmid[g, rows], tr[g, 1, rows]

    outs = []

    def emit(position, flag, stay, other=None):
        rows = pl.ds(position * BLOCK, BLOCK)
        values = parts(stay)
        if other is not None:
            values = [pick(flag, a, b) for a, b in zip(values, parts(other))]
        obuf[rows, :BLOCK] = values[0]
        obuf[rows, BLOCK:3 * BLOCK] = values[1]
        obuf[rows, 3 * BLOCK:] = values[2]
        copy = pltpu.make_async_copy(obuf.at[rows], out_ref.at[rows], out_sem.at[position])
        copy.start()
        outs.append(copy)

    def await_group(g):
        for side in range(2):
            await_side(g, side, ts, tr, tx_s, tx_r)

    await_group(0)
    emit(4, None, 3)
    await_group(1)
    emit(3, None, 4)
    await_group(2)
    emit(1, finals[0], 1, 2)
    emit(2, finals[0], 2, 1)
    emit(5, finals[1], 5, 6)
    emit(6, finals[1], 6, 5)
    await_group(3)
    emit(0, None, 0)
    emit(7, None, 7)

    for copy in started:
        copy.wait_send()
    for t in range(2):
        for h in range(2):
            src = rot_ref.at[t, pl.ds(2 * h, 2)]
            dst = rc.at[t, :, row_from // Z, row_from % Z, core]
            there = remote(src, dst, tr_s.at[t, h], tr_r.at[t, core], across[h])

            @pl.when(jnp.logical_not(stays[h]))
            def _():
                there.wait_send()

    for table in (x_copies, t_copies):
        for to_left, to_right in table.values():
            @pl.when(has_left)
            def _():
                to_left.wait_send()

            @pl.when(has_right)
            def _():
                to_right.wait_send()

    for table in (vx, ux):
        for copy, has in table.values():
            @pl.when(has)
            def _():
                copy.wait_send()

    for copy in outs:
        copy.wait()


def body(covariance, rotations, pairing):
    dma = pltpu.SemaphoreType.DMA
    tile = covariance.shape
    scratch = [
        pltpu.VMEM(tile, F32),
        pltpu.VMEM((2, RP, Y, XH, CORE, 8, PAIR), F32),
        pltpu.VMEM((2, 2, XL, Z, 2, 8, PAIR), F32),
        pltpu.VMEM((2, RP, 2, PAIR, PAIR), B16),
        pltpu.VMEM((2, 2, 2, PAIR, PAIR), B16),
        pltpu.VMEM((4, 2, PAIR, BLOCK), F32),
        pltpu.VMEM((4, 2, PAIR, BLOCK), F32),
        pltpu.VMEM((tile[0], PAIR), F32),
        pltpu.VMEM((2, RB, BLOCK, PAIR), F32),
        pltpu.VMEM((2, 2, BLOCK, PAIR), F32),
        pltpu.VMEM((2, RB, BLOCK, PAIR), F32),
        pltpu.VMEM((2, 2, BLOCK, PAIR), F32),
        pltpu.VMEM((4, 2, PAIR, BLOCK), F32),
        pltpu.VMEM((4, 2, PAIR, BLOCK), F32),
        pltpu.VMEM((4, PAIR, PAIR), F32),
        pltpu.VMEM(tile, F32),
        dma((3,)),
        dma((2, 2)), dma((2, 2)),
        dma((2,)), dma((2,)),
        dma((2,)), dma((2,)),
        dma((2, 2, 4)), dma((2, 2, 4)),
        dma((2, 2, 4)), dma((2, 2, 4)),
        dma((2, Y)), dma((2, Y)),
        dma((4, 2)), dma((4, 2)),
        dma((2, 2)), dma((2, 2)),
        dma((2, 2)), dma((2, 2)),
        dma((4, 2)), dma((4, 2)),
        dma((RB,)),
    ]
    return pl.pallas_call(
        kernel,
        out_shape=jax.ShapeDtypeStruct(tile, F32),
        in_specs=[
            pl.BlockSpec(memory_space=pl.ANY),
            pl.BlockSpec(memory_space=pl.ANY),
            pl.BlockSpec(memory_space=pltpu.SMEM),
        ],
        out_specs=pl.BlockSpec(memory_space=pl.ANY),
        scratch_shapes=scratch,
        compiler_params=pltpu.CompilerParams(
            collective_id=0, has_side_effects=True, vmem_limit_bytes=48 * 2**20
        ),
        cost_estimate=pl.CostEstimate(
            flops=2 * 4 * tile[0] * tile[1] * PAIR, bytes_accessed=8 * tile[0] * tile[1],
            transcendentals=0,
        ),
    )(covariance, rotations, pairing)


def solution(mesh):
    in_specs = (P("row", "col"), P(None, "row", "col", None), P())
    out_specs = P("row", "col")
    return jax.shard_map(body, mesh=mesh, in_specs=in_specs, out_specs=out_specs, check_vma=False)
```

time: 479 us -> 105 us (0.22)
  the two profiles are of different devices: /device:TPU:35 before, /device:TPU:9 now
where the time goes in v1:
time: 105 us
  Pallas kernels  101 us (96%)
  local copies, waits for them, and re-layouts  4.43 us (4%)
    pallas_call x1, Pallas kernels, body(): pl.pallas_call(kernel, out_shape=jax.ShapeDtypeStruct(tile, F32), in_spec...  101 us
    unnamed x7, local copies, waits for them, and re-layouts  4.43 us

profile of v1, /device:TPU:9, one launch (start us, length us, event | category | flops | bytes accessed | tf_op | source)
XLA Modules:
  0.0 105.3 jit_solution(9831816628034900709)
XLA Ops:
  0.0 0.0 copy-start
  0.0 1.6 %copy-done = f32[1024,512]{1,0:T(8,128)S(1)} copy-done((f32[1024,512]{1,0:T(8,128)S(1)}, f32[1024,512]{1,0:T(8,128)}, u32[]{:S(2)}) %copy-start) | copy-done | bytes 2097176
  1.6 0.0 copy-start.1
  1.6 0.8 copy-done.1
  2.4 0.0 copy-start.2
  2.4 0.7 copy-done.2
  3.1 100.8 %shard_map.37 = f32[1024,512]{1,0:T(8,128)S(1)} custom-call(f32[1024,512]{1,0:T(8,128)S(1)} %copy-done, f32[2,4,8,256]{3,2,1,0:T(8,128)S(1)} %copy-done.1, s32[2,128]{1,0:T(2,128)S(1)} %copy-done.2), custom_call_target="tpu_custom_call" | custom-call | flops 1073741824 | bytes 4194304 | tf_op jit(solution)/shard_map/pallas_call | solution.py:476
  103.9 1.3 %copy.5 = f32[1024,512]{1,0:T(8,128)} copy(f32[1024,512]{1,0:T(8,128)S(1)} %shard_map.37) | data formatting | bytes 4194304
Async XLA Ops:
  0.0 1.6 %copy-start = (f32[1024,512]{1,0:T(8,128)S(1)}, f32[1024,512]{1,0:T(8,128)}, u32[]{:S(2)}) copy-start(f32[1024,512]{1,0:T(8,128)} %cov_ref.1) | copy-start | bytes 6291460
  1.6 0.8 copy-start.1
  2.4 0.7 copy-start.2

commit v2 on v0

v2 whole, which is shorter than its diff:
```python
import jax
import jax.numpy as jnp
from jax import lax
from jax.experimental import pallas as pl
from jax.experimental.pallas import tpu as pltpu
from jax.sharding import PartitionSpec as P

BLOCK = 128
PAIR = 2 * BLOCK
ROWS, COLS = 16, 32
XL, Z, Y, XH, CORE = 2, 8, 8, 2, 2
RB, CB = 8, 4
RP = RB // 2
MESH = pl.DeviceIdType.MESH
F32, B16 = jnp.float32, jnp.bfloat16


def split(value):
    high = value.astype(B16)
    low = (value - high.astype(F32)).astype(B16)
    return high, low


def dot(a, b):
    return jnp.dot(a, b, preferred_element_type=F32)


def dot3(a, b):
    return dot(a[0], b[0]) + (dot(a[0], b[1]) + dot(a[1], b[0]))


def kernel(
    cov_ref, rot_ref, pair_ref, out_ref,
    cbuf, rr, rc, rrt, rcs, v, vr, u, ur, xs, xr, xmid, ts, tr, tmid, obuf,
    loc_sem, tr_s, tr_r, xl_s, xl_r, xh_s, xh_r, z_s, z_r, y_s, y_r, mt_s, mt_r,
    vx_s, vx_r, ux_s, ux_r, cx_s, cx_r, tx_s, tx_r, out_sem,
):
    r = lax.axis_index("row")
    c = lax.axis_index("col")
    xl, z = r // Z, r % Z
    y, xh, core = c // 4, (c // 2) % 2, c % 2

    def z_dev(step):
        return (xl * Z + (z + step + Z) % Z, c)

    def y_dev(step):
        return (r, ((y + step + Y) % Y) * 4 + xh * 2 + core)

    mate = (r, y * 4 + xh * 2 + (1 - core))
    xh_mate = (r, y * 4 + (1 - xh) * 2 + core)
    xl_mate = ((1 - xl) * Z + z, c)
    up = ((r + ROWS - 1) % ROWS, c)
    down = ((r + 1) % ROWS, c)
    left = (r, (c + COLS - 1) % COLS)
    right = (r, (c + 1) % COLS)
    across = [(c // 2, 2 * r + h) for h in range(2)]
    diagonal = c // 2 == r
    stays = [jnp.logical_and(diagonal, core == h) for h in range(2)]
    ends = ((0, up, r > 0), (RB - 1, down, r < ROWS - 1))
    sides = ((left, c > 0), (right, c < COLS - 1))

    def remote(src, dst, send, recv, device):
        return pltpu.make_async_remote_copy(
            src_ref=src, dst_ref=dst, send_sem=send, recv_sem=recv,
            device_id=device, device_id_type=MESH,
        )

    started = []

    def go(copy):
        copy.start()
        started.append(copy)

    def arrived(ref, recv):
        remote(ref, ref, loc_sem.at[0], recv, mate).wait_recv()

    load = pltpu.make_async_copy(cov_ref, cbuf, loc_sem.at[0])
    load.start()
    own = [
        pltpu.make_async_copy(rot_ref.at[t], rr.at[t, :, y, xh, core], loc_sem.at[1 + t])
        for t in range(2)
    ]
    for t in range(2):
        own[t].start()

    barrier = pltpu.get_barrier_semaphore()
    peers = [mate, xh_mate, xl_mate, up, down, left, right]
    peers += [dev(step) for dev in (z_dev, y_dev) for step in (1, -1, 2, -2)]
    for peer in peers:
        pl.semaphore_signal(barrier, inc=1, device_id=peer, device_id_type=MESH)
    for h in range(2):
        @pl.when(jnp.logical_not(stays[h]))
        def _():
            pl.semaphore_signal(barrier, inc=1, device_id=across[h], device_id_type=MESH)
    pl.semaphore_wait(barrier, len(peers) + jnp.where(diagonal, 1, 2))

    def across_copy(t, h):
        src = rot_ref.at[t, pl.ds(2 * h, 2)]
        dst = rc.at[t, :, c // 2 // Z, c // 2 % Z, core]
        there = remote(src, dst, tr_s.at[t, h], tr_r.at[t, core], across[h])
        here = pltpu.make_async_copy(src, dst, tr_r.at[t, core])
        return there, here

    def across_send(t):
        for h in range(2):
            there, here = across_copy(t, h)

            @pl.when(stays[h])
            def _():
                here.start()

            @pl.when(jnp.logical_not(stays[h]))
            def _():
                there.start()

    def y_block(t, origin, half=None):
        if half is None:
            return rr.at[t, :, origin, xh, core]
        return rr.at[t, pl.ds(2 * half, 2), origin, xh, core]

    def z_block(t, origin, half=None):
        if half is None:
            return rc.at[t, :, :, origin]
        return rc.at[t, :, half, origin]

    STEPS = (1, -1, 2, -2, 3, -3)

    def spread_rows(t, origin, src=None):
        ref = y_block(t, origin)
        src = ref if src is None else src
        go(remote(src, ref, xh_s.at[t, origin], xh_r.at[t, origin], xh_mate))
        go(remote(src, ref, mt_s.at[t, origin, 0], mt_r.at[t, origin, xh], mate))

    def first_level(block, t, me, send, recv, dev, src=None):
        ref = block(t, me)
        src = ref if src is None else src
        for i in range(4):
            go(remote(src, ref, send.at[t, i], recv.at[t, i], dev(STEPS[i])))

    def second_level(block, t, me, n, send, recv, dev, then=None):
        for i in (2, 3):
            way = 1 if i == 2 else -1
            origin = (me - 2 * way + n) % n
            ref = block(t, origin)
            arrived(ref, recv.at[t, i])
            go(remote(ref, ref, send.at[t, i + 2], recv.at[t, i + 2], dev(way)))
            part = block(t, origin, i - 2)
            go(remote(part, part, send.at[t, i + 4], recv.at[t, i + 4], dev(2 * way)))
            if then is not None:
                then(t, origin)
        for i in (0, 1):
            origin = (me - STEPS[i] + n) % n
            arrived(block(t, origin), recv.at[t, i])
            if then is not None:
                then(t, origin)

    def third_level(block, t, me, n, recv, then=None):
        for i in (4, 5):
            origin = (me - STEPS[i] + n) % n
            arrived(block(t, origin), recv.at[t, i])
            if then is not None:
                then(t, origin)
        origin = (me + n // 2) % n
        for half in range(2):
            arrived(block(t, origin, half), recv.at[t, 6 + half])
        if then is not None:
            then(t, origin)

    def y_first(t):
        piece = rot_ref.at[t]
        first_level(y_block, t, y, y_s, y_r, y_dev, piece)
        spread_rows(t, y, piece)

    def y_second(t):
        second_level(y_block, t, y, Y, y_s, y_r, y_dev, spread_rows)

    def y_third(t):
        third_level(y_block, t, y, Y, y_r, spread_rows)

    def x_pass(t):
        for step in (0, 1, -1, 2, -2, 3, -3, 4):
            origin = (y + step + Y) % Y
            ref = rr.at[t, :, origin, 1 - xh, core]
            arrived(ref, xh_r.at[t, origin])
            go(remote(ref, ref, mt_s.at[t, origin, 1], mt_r.at[t, origin, 1 - xh], mate))

    def mate_wait(t):
        for origin in range(Y):
            for side in range(2):
                arrived(rr.at[t, :, origin, side, 1 - core], mt_r.at[t, origin, side])
        own[t].wait()

    def z_begin(t):
        for s in range(2):
            arrived(rc.at[t, :, xl, z, s], tr_r.at[t, s])
        ref = rc.at[t, :, xl, z]
        go(remote(ref, ref, xl_s.at[t], xl_r.at[t], xl_mate))

    def z_first(t):
        arrived(rc.at[t, :, 1 - xl, z], xl_r.at[t])
        first_level(z_block, t, z, z_s, z_r, z_dev)

    def z_second(t):
        second_level(z_block, t, z, Z, z_s, z_r, z_dev)

    def z_third(t):
        third_level(z_block, t, z, Z, z_r)

    def split_cols(t):
        for k in range(2):
            high, low = split(rc[t, k].reshape(PAIR, PAIR))
            rcs[t, k, 0] = high
            rcs[t, k, 1] = low

    def split_rows(t):
        def one(k, _):
            high, low = split(rr[t, k].reshape(PAIR, PAIR).T)
            rrt[t, k, 0] = high
            rrt[t, k, 1] = low
            return 0
        lax.fori_loop(0, RP, one, 0)

    def col_flag(t):
        return pair_ref[t, c * CB + 1] - (c * CB + 1)

    def row_flag(t, which):
        first = r * RB + 1 + 4 * which
        return pair_ref[t, first] - first

    def pick(flag, stay, other):
        return jnp.where(jnp.full(stay.shape, flag, jnp.int32) != 0, other, stay)

    def mix_rows(t, k, value, buf):
        out = dot3((rrt[t, k, 0], rrt[t, k, 1]), split(value))
        buf[2 * k] = out[:BLOCK]
        buf[2 * k + 1] = out[BLOCK:]

    row_copies = []

    def send_row(buf, got, send, recv, which):
        edge, device, has = ends[which]
        copy = remote(buf.at[edge], got.at[1 - which], send.at[which], recv.at[1 - which], device)
        row_copies.append((copy, has))

        @pl.when(has)
        def _():
            copy.start()

    def await_row(buf, got, recv, which):
        edge, device, has = ends[which]

        @pl.when(has)
        def _():
            arrived(got.at[which], recv.at[which])

        @pl.when(jnp.logical_not(has))
        def _():
            got[which] = buf[edge]

    flags = [row_flag(0, 0), row_flag(0, 1)]

    def second_rows(k):
        if k == 0:
            pair = (vr[0], pick(flags[0], v[1], v[2]))
        elif k == 1:
            pair = (pick(flags[0], v[2], v[1]), v[4])
        elif k == 2:
            pair = (v[3], pick(flags[1], v[5], v[6]))
        else:
            pair = (pick(flags[1], v[6], v[5]), vr[1])
        mix_rows(1, k, jnp.concatenate(pair, axis=0), u)

    groups = (((u, 2), (u, 3)), ((u, 4), (u, 5)), ((u, 1), (u, 6)), ((ur, 0), (ur, 1)))
    side_copies = []

    def mix_cols(t, g, first, second, outer, middle, got, send, recv):
        one = dot3(split(first), (rcs[t, 0, 0], rcs[t, 0, 1]))
        outer[g, 0] = one[:, :BLOCK]
        two = dot3(split(second), (rcs[t, 1, 0], rcs[t, 1, 1]))
        outer[g, 1] = two[:, BLOCK:]
        for side, (device, has) in enumerate(sides):
            copy = remote(
                outer.at[g, side], got.at[g, 1 - side],
                send.at[g, side], recv.at[g, 1 - side], device,
            )
            side_copies.append((copy, has))

            @pl.when(has)
            def _():
                copy.start()

        flag = col_flag(t)
        b1, b2 = one[:, BLOCK:], two[:, :BLOCK]
        middle[g, :, :BLOCK] = pick(flag, b1, b2)
        middle[g, :, BLOCK:] = pick(flag, b2, b1)

    def await_sides(g, outer, got, recv):
        for side, (device, has) in enumerate(sides):
            @pl.when(has)
            def _():
                arrived(got.at[g, side], recv.at[g, side])

            @pl.when(jnp.logical_not(has))
            def _():
                got[g, side] = outer[g, side]

    def first_cols(g):
        rows = jnp.concatenate([buf[i] for buf, i in groups[g]], axis=0)
        mix_cols(0, g, rows[:, :PAIR], rows[:, PAIR:], xs, xmid, xr, cx_s, cx_r)

    def second_cols(g):
        await_sides(g, xs, xr, cx_r)
        first = jnp.concatenate((xr[g, 0], xmid[g, :, :BLOCK]), axis=1)
        second = jnp.concatenate((xmid[g, :, BLOCK:], xr[g, 1]), axis=1)
        mix_cols(1, g, first, second, ts, tmid, tr, tx_s, tx_r)

    across_send(0)
    y_first(0)
    across_send(1)
    y_first(1)
    y_second(0)
    y_second(1)
    z_begin(0)
    z_first(0)
    y_third(0)
    z_begin(1)
    y_third(1)
    x_pass(0)
    z_second(0)
    z_first(1)
    mate_wait(0)
    load.wait()

    split_rows(0)
    for k in (0, 3, 1, 2):
        mix_rows(0, k, cbuf[pl.ds(k * PAIR, PAIR), :], v)
        if k in (0, 3):
            send_row(v, vr, vx_s, vx_r, k // 3)
    x_pass(1)
    z_third(0)
    split_cols(0)
    z_second(1)
    mate_wait(1)
    split_rows(1)
    second_rows(1)
    first_cols(0)
    second_rows(2)
    first_cols(1)
    for which, k in ((0, 0), (1, 3)):
        await_row(v, vr, vx_r, which)
        second_rows(k)
        send_row(u, ur, ux_s, ux_r, which)
    first_cols(2)
    z_third(1)
    split_cols(1)
    second_cols(0)
    second_cols(1)
    for which in range(2):
        await_row(u, ur, ux_r, which)
    first_cols(3)
    second_cols(2)
    second_cols(3)

    places = {1: (2, 0), 2: (0, 0), 3: (0, 1), 4: (1, 0), 5: (1, 1), 6: (2, 1), 0: (3, 0), 7: (3, 1)}
    finals = [row_flag(1, 0), row_flag(1, 1)]

    def parts(block):
        g, half = places[block]
        rows = pl.ds(half * BLOCK, BLOCK)
        return tr[g, 0, rows], tmid[g, rows], tr[g, 1, rows]

    outs = []

    def emit(position, flag, stay, other=None):
        rows = pl.ds(position * BLOCK, BLOCK)
        values = parts(stay)
        if other is not None:
            values = [pick(flag, a, b) for a, b in zip(values, parts(other))]
        obuf[rows, :BLOCK] = values[0]
        obuf[rows, BLOCK:3 * BLOCK] = values[1]
        obuf[rows, 3 * BLOCK:] = values[2]
        copy = pltpu.make_async_copy(obuf.at[rows], out_ref.at[rows], out_sem.at[position])
        copy.start()
        outs.append(copy)

    await_sides(0, ts, tr, tx_r)
    emit(4, None, 3)
    await_sides(1, ts, tr, tx_r)
    emit(3, None, 4)
    await_sides(2, ts, tr, tx_r)
    emit(1, finals[0], 1, 2)
    emit(2, finals[0], 2, 1)
    emit(5, finals[1], 5, 6)
    emit(6, finals[1], 6, 5)
    await_sides(3, ts, tr, tx_r)
    emit(0, None, 0)
    emit(7, None, 7)

    for copy in started:
        copy.wait_send()
    for t in range(2):
        for h in range(2):
            there, here = across_copy(t, h)

            @pl.when(jnp.logical_not(stays[h]))
            def _():
                there.wait_send()

    for copy, has in row_copies + side_copies:
        @pl.when(has)
        def _():
            copy.wait_send()

    for copy in outs:
        copy.wait()


def body(covariance, rotations, pairing):
    dma = pltpu.SemaphoreType.DMA
    tile = covariance.shape
    wide = (BLOCK, tile[1])
    outer = pltpu.VMEM((4, 2, PAIR, BLOCK), F32)
    middle = pltpu.VMEM((4, PAIR, PAIR), F32)
    scratch = [
        pltpu.VMEM(tile, F32),
        pltpu.VMEM((2, RP, Y, XH, CORE, 8, PAIR), F32),
        pltpu.VMEM((2, 2, XL, Z, 2, 8, PAIR), F32),
        pltpu.VMEM((2, RP, 2, PAIR, PAIR), B16),
        pltpu.VMEM((2, 2, 2, PAIR, PAIR), B16),
        pltpu.VMEM((RB, *wide), F32),
        pltpu.VMEM((2, *wide), F32),
        pltpu.VMEM((RB, *wide), F32),
        pltpu.VMEM((2, *wide), F32),
        outer, outer, middle,
        outer, outer, middle,
        pltpu.VMEM(tile, F32),
        dma((3,)),
        dma((2, 2)), dma((2, 2)),
        dma((2,)), dma((2,)),
        dma((2, Y)), dma((2, Y)),
        dma((2, 8)), dma((2, 8)),
        dma((2, 8)), dma((2, 8)),
        dma((2, Y, 2)), dma((2, Y, 2)),
        dma((2,)), dma((2,)),
        dma((2,)), dma((2,)),
        dma((4, 2)), dma((4, 2)),
        dma((4, 2)), dma((4, 2)),
        dma((RB,)),
    ]
    return pl.pallas_call(
        kernel,
        out_shape=jax.ShapeDtypeStruct(tile, F32),
        in_specs=[
            pl.BlockSpec(memory_space=pltpu.HBM),
            pl.BlockSpec(memory_space=pltpu.HBM),
            pl.BlockSpec(memory_space=pltpu.SMEM),
        ],
        out_specs=pl.BlockSpec(memory_space=pl.ANY),
        scratch_shapes=scratch,
        compiler_params=pltpu.CompilerParams(
            collective_id=0, has_side_effects=True, vmem_limit_bytes=60 * 2**20
        ),
        cost_estimate=pl.CostEstimate(
            flops=2 * 4 * tile[0] * tile[1] * PAIR, bytes_accessed=8 * tile[0] * tile[1],
            transcendentals=0,
        ),
    )(covariance, rotations, pairing)


def solution(mesh):
    in_specs = (P("row", "col"), P(None, "row", "col", None), P())
    out_specs = P("row", "col")
    return jax.shard_map(body, mesh=mesh, in_specs=in_specs, out_specs=out_specs, check_vma=False)
```

time: 479 us -> 87.5 us (0.18)
  the two profiles are of different devices: /device:TPU:35 before, /device:TPU:1 now
where the time goes in v2:
time: 87.5 us; the launch traced here: 87.4 us
  Pallas kernels  84.3 us (96%)
  local copies, waits for them, and re-layouts  3.08 us (4%)
    pallas_call x1, Pallas kernels, body(): pl.pallas_call(kernel, out_shape=jax.ShapeDtypeStruct(tile, F32), in_spec...  84.3 us
    unnamed x1, local copies, waits for them, and re-layouts  3.08 us

profile of v2, /device:TPU:1, one launch (start us, length us, event | category | flops | bytes accessed | tf_op | source)
XLA Modules:
  0.0 87.4 jit_solution(5573832473070715532)
XLA Ops:
  0.0 84.3 %shard_map.37 = f32[1024,512]{1,0:T(8,128)} custom-call(f32[1024,512]{1,0:T(8,128)} %cov_ref.1, f32[2,4,8,256]{3,2,1,0:T(8,128)} %rot_ref.1, s32[2,128]{1,0:T(2,128)} %pair_ref.1), custom_call_target="tpu_custom_call" | custom-call | flops 1073741824 | bytes 4194304 | tf_op jit(solution)/shard_map/pallas_call | solution.py:450
  84.3 3.1 %copy.5 = f32[1024,512]{1,0:T(8,128)} copy(f32[1024,512]{1,0:T(8,128)} %shard_map.37) | data formatting | bytes 4194304

commit v3 on v2

v3 whole, which is shorter than its diff:
```python
import jax
import jax.numpy as jnp
from jax import lax
from jax.experimental import pallas as pl
from jax.experimental.pallas import tpu as pltpu
from jax.sharding import PartitionSpec as P

BLOCK = 128
PAIR = 2 * BLOCK
ROWS, COLS = 16, 32
XL, Z, Y, XH, CORE = 2, 8, 8, 2, 2
RB, CB = 8, 4
RP = RB // 2
MESH = pl.DeviceIdType.MESH
F32, B16 = jnp.float32, jnp.bfloat16


def split(value):
    high = value.astype(B16)
    low = (value - high.astype(F32)).astype(B16)
    return high, low


def dot(a, b):
    return jnp.dot(a, b, preferred_element_type=F32)


def dot3(a, b):
    return dot(a[0], b[0]) + (dot(a[0], b[1]) + dot(a[1], b[0]))


def kernel(
    cov_ref, rot_ref, pair_ref, out_ref,
    cbuf, halo, rr, rc0, rc, rrt, qs, rcs, w, v, vr, u, ur, ts, tr, tmid, obuf,
    loc_sem, h_s, h_r, t0_s, t0_r, tr_s, tr_r, xl_s, xl_r, xh_s, xh_r, z_s, z_r, y_s, y_r, mt_s, mt_r,
    vx_s, vx_r, ux_s, ux_r, tx_s, tx_r, out_sem,
):
    r = lax.axis_index("row")
    c = lax.axis_index("col")
    xl, z = r // Z, r % Z
    y, xh, core = c // 4, (c // 2) % 2, c % 2

    def z_dev(step):
        return (xl * Z + (z + step + Z) % Z, c)

    def y_dev(step):
        return (r, ((y + step + Y) % Y) * 4 + xh * 2 + core)

    mate = (r, y * 4 + xh * 2 + (1 - core))
    xh_mate = (r, y * 4 + (1 - xh) * 2 + core)
    xl_mate = ((1 - xl) * Z + z, c)
    up = ((r + ROWS - 1) % ROWS, c)
    down = ((r + 1) % ROWS, c)
    left = (r, (c + COLS - 1) % COLS)
    right = (r, (c + 1) % COLS)
    across = [(c // 2, 2 * r + h) for h in range(2)]
    diagonal = c // 2 == r
    stays = [jnp.logical_and(diagonal, core == h) for h in range(2)]
    ends = ((0, up, r > 0), (RB - 1, down, r < ROWS - 1))
    sides = ((left, c > 0), (right, c < COLS - 1))

    def remote(src, dst, send, recv, device):
        return pltpu.make_async_remote_copy(
            src_ref=src, dst_ref=dst, send_sem=send, recv_sem=recv,
            device_id=device, device_id_type=MESH,
        )

    started = []

    def go(copy):
        copy.start()
        started.append(copy)

    def arrived(ref, recv):
        remote(ref, ref, loc_sem.at[0], recv, mate).wait_recv()

    load = pltpu.make_async_copy(cov_ref, cbuf, loc_sem.at[0])
    load.start()
    own = [
        pltpu.make_async_copy(rot_ref.at[t], rr.at[t, :, y, xh, core], loc_sem.at[1 + t])
        for t in range(2)
    ]
    for t in range(2):
        own[t].start()

    barrier = pltpu.get_barrier_semaphore()
    peers = [mate, xh_mate, xl_mate, up, down, left, right]
    peers += [dev(step) for dev in (z_dev, y_dev) for step in (1, -1, 2, -2)]
    for peer in peers:
        pl.semaphore_signal(barrier, inc=1, device_id=peer, device_id_type=MESH)
    beside = c // 2 + jnp.where(core == 0, -1, 1)
    has_beside = jnp.logical_and(beside >= 0, beside < ROWS)
    for s in range(2):
        @pl.when(jnp.logical_not(jnp.logical_and(diagonal, core == s)))
        def _():
            pl.semaphore_signal(barrier, inc=1, device_id=(c // 2, 2 * r + s), device_id_type=MESH)

        @pl.when(has_beside)
        def _():
            pl.semaphore_signal(
                barrier, inc=1, device_id=((beside + ROWS) % ROWS, 2 * r + s), device_id_type=MESH
            )
    targets = 2 + jnp.where(r > 0, 1, 0) + jnp.where(r < ROWS - 1, 1, 0) - jnp.where(diagonal, 1, 0)
    pl.semaphore_wait(barrier, len(peers) + targets)

    def halo_send(k):
        rows = pl.ds(k * PAIR, PAIR)
        for side, (device, has) in enumerate(sides):
            src = cov_ref.at[rows, pl.ds(side * PAIR, PAIR)]
            copy = remote(src, halo.at[1 - side, rows], h_s.at[k, side], h_r.at[k, 1 - side], device)
            here = pltpu.make_async_copy(src, halo.at[side, rows], h_r.at[k, side])
            side_copies.append((copy, has))

            @pl.when(has)
            def _():
                copy.start()

            @pl.when(jnp.logical_not(has))
            def _():
                here.start()

    def halo_wait(k):
        for side in range(2):
            arrived(halo.at[side, pl.ds(k * PAIR, PAIR)], h_r.at[k, side])

    side_copies = []

    first_tile = jnp.where(r > 0, 2 * r - 1, 0)
    last_tile = jnp.where(r < ROWS - 1, 2 * r + 2, COLS - 1)
    pieces = (
        (0, 0, first_tile, jnp.where(r > 0, 3, 0)),
        (0, 1, 2 * r, 1), (1, 0, 2 * r, 2), (2, 0, 2 * r, 3),
        (1, 1, 2 * r + 1, 0), (2, 1, 2 * r + 1, 1), (3, 0, 2 * r + 1, 2),
        (3, 1, last_tile, jnp.where(r < ROWS - 1, 0, 3)),
    )
    piece_copies = []

    def pieces_send():
        for i, (k, half, tile, position) in enumerate(pieces):
            src = rot_ref.at[0, k, :, pl.ds(half * BLOCK, BLOCK)]
            dst = rc0.at[position, c // 2 // Z, c // 2 % Z, core]
            there = remote(src, dst, t0_s.at[i], t0_r.at[position, core], (c // 2, tile))
            here = pltpu.make_async_copy(src, dst, t0_r.at[position, core])
            away = jnp.logical_not(jnp.logical_and(diagonal, tile == c))
            piece_copies.append((there, away))

            @pl.when(away)
            def _():
                there.start()

            @pl.when(jnp.logical_not(away))
            def _():
                here.start()

    def across_copy(h):
        src = rot_ref.at[1, pl.ds(2 * h, 2)]
        dst = rc.at[:, c // 2 // Z, c // 2 % Z, core]
        there = remote(src, dst, tr_s.at[h], tr_r.at[core], across[h])
        here = pltpu.make_async_copy(src, dst, tr_r.at[core])
        return there, here

    def across_send():
        for h in range(2):
            there, here = across_copy(h)

            @pl.when(stays[h])
            def _():
                here.start()

            @pl.when(jnp.logical_not(stays[h]))
            def _():
                there.start()

    def y_block(t, origin, half=None):
        if half is None:
            return rr.at[t, :, origin, :, core]
        return rr.at[t, :, origin, half, core]

    def z_block(t, origin, half=None):
        if t == 0:
            return rc0.at[:, :, origin] if half is None else rc0.at[:, half, origin]
        return rc.at[:, :, origin] if half is None else rc.at[:, half, origin]

    STEPS = (1, -1, 2, -2, 3, -3)

    def first_level(block, t, me, send, recv, dev, src=None):
        ref = block(t, me)
        src = ref if src is None else src
        for i in (2, 3, 0, 1):
            go(remote(src, ref, send.at[t, i], recv.at[t, i], dev(STEPS[i])))

    def second_level(block, t, me, n, send, recv, dev, then=None):
        for i in (2, 3):
            way = 1 if i == 2 else -1
            origin = (me - 2 * way + n) % n
            ref = block(t, origin)
            arrived(ref, recv.at[t, i])
            part = block(t, origin, i - 2)
            go(remote(part, part, send.at[t, i + 4], recv.at[t, i + 4], dev(2 * way)))
            go(remote(ref, ref, send.at[t, i + 2], recv.at[t, i + 2], dev(way)))
            if then is not None:
                then(t, origin)
        for i in (0, 1):
            origin = (me - STEPS[i] + n) % n
            arrived(block(t, origin), recv.at[t, i])
            if then is not None:
                then(t, origin)

    def third_level(block, t, me, n, recv, then=None):
        for i in (4, 5):
            origin = (me - STEPS[i] + n) % n
            arrived(block(t, origin), recv.at[t, i])
            if then is not None:
                then(t, origin)
        origin = (me + n // 2) % n
        for half in range(2):
            arrived(block(t, origin, half), recv.at[t, 6 + half])
        if then is not None:
            then(t, origin)

    def y_begin(t):
        go(remote(rot_ref.at[t], rr.at[t, :, y, xh, core], xh_s.at[t], xh_r.at[t], xh_mate))

    def y_first(t):
        own[t].wait()
        arrived(rr.at[t, :, y, 1 - xh, core], xh_r.at[t])
        first_level(y_block, t, y, y_s, y_r, y_dev)

    def y_second(t):
        second_level(y_block, t, y, Y, y_s, y_r, y_dev)

    def y_third(t):
        third_level(y_block, t, y, Y, y_r)
        ref = rr.at[t, :, :, :, core]
        go(remote(ref, ref, mt_s.at[t], mt_r.at[t], mate))

    def mate_wait(t):
        arrived(rr.at[t, :, :, :, 1 - core], mt_r.at[t])

    def z_begin(t):
        for s in range(2):
            if t == 0:
                for position in range(CB):
                    arrived(rc0.at[position, xl, z, s], t0_r.at[position, s])
            else:
                arrived(rc.at[:, xl, z, s], tr_r.at[s])
        ref = rc0.at[:, xl, z] if t == 0 else rc.at[:, xl, z]
        go(remote(ref, ref, xl_s.at[t], xl_r.at[t], xl_mate))

    def z_first(t):
        buf = rc0 if t == 0 else rc
        arrived(buf.at[:, 1 - xl, z], xl_r.at[t])
        first_level(z_block, t, z, z_s, z_r, z_dev)

    def z_second(t):
        second_level(z_block, t, z, Z, z_s, z_r, z_dev)

    def z_third(t):
        third_level(z_block, t, z, Z, z_r)

    def split_first():
        for position in range(CB):
            high, low = split(rc0[position].reshape(PAIR, BLOCK))
            qs[position, 0] = high
            qs[position, 1] = low

    def split_second():
        for k in range(2):
            high, low = split(rc[k].reshape(PAIR, PAIR))
            rcs[k, 0] = high
            rcs[k, 1] = low

    def split_rows(t):
        def one(k, _):
            high, low = split(rr[t, k].reshape(PAIR, PAIR).T)
            rrt[t, k, 0] = high
            rrt[t, k, 1] = low
            return 0
        lax.fori_loop(0, RP, one, 0)

    def col_flag(t):
        return pair_ref[t, c * CB + 1] - (c * CB + 1)

    def row_flag(t, which):
        first = r * RB + 1 + 4 * which
        return pair_ref[t, first] - first

    def pick(flag, stay, other):
        return jnp.where(jnp.full(stay.shape, flag, jnp.int32) != 0, other, stay)

    def mix_rows(t, k, value, buf, cols=slice(None)):
        out = dot3((rrt[t, k, 0], rrt[t, k, 1]), split(value))
        buf[2 * k, :, cols] = out[:BLOCK]
        buf[2 * k + 1, :, cols] = out[BLOCK:]

    row_copies = []
    HALVES = [pl.ds(half * PAIR, PAIR) for half in range(2)]

    def send_row(buf, got, send, recv, which, half):
        edge, device, has = ends[which]
        copy = remote(
            buf.at[edge, :, HALVES[half]], got.at[1 - which, :, HALVES[half]],
            send.at[half, which], recv.at[half, 1 - which], device,
        )
        row_copies.append((copy, has))

        @pl.when(has)
        def _():
            copy.start()

    def await_row(buf, got, recv, which, half):
        edge, device, has = ends[which]
        cols = HALVES[half]

        @pl.when(has)
        def _():
            arrived(got.at[which, :, cols], recv.at[half, which])

        @pl.when(jnp.logical_not(has))
        def _():
            got[which, :, cols] = buf[edge, :, cols]

    flags = [row_flag(0, 0), row_flag(0, 1)]

    def second_rows(k, cols=slice(None)):
        if k == 0:
            pair = (vr[0, :, cols], pick(flags[0], v[1, :, cols], v[2, :, cols]))
        elif k == 1:
            pair = (pick(flags[0], v[2, :, cols], v[1, :, cols]), v[4, :, cols])
        elif k == 2:
            pair = (v[3, :, cols], pick(flags[1], v[5, :, cols], v[6, :, cols]))
        else:
            pair = (pick(flags[1], v[6, :, cols], v[5, :, cols]), vr[1, :, cols])
        mix_rows(1, k, jnp.concatenate(pair, axis=0), u, cols)

    def first_cols(k):
        rows = pl.ds(k * PAIR, PAIR)
        halo_wait(k)
        values = (halo[0, rows], cbuf[rows, :PAIR], cbuf[rows, PAIR:], halo[1, rows])
        out = [dot3(split(value), (qs[p, 0], qs[p, 1])) for p, value in enumerate(values)]
        flag = col_flag(0)
        w[rows, :BLOCK] = out[0]
        w[rows, BLOCK:2 * BLOCK] = pick(flag, out[1], out[2])
        w[rows, 2 * BLOCK:3 * BLOCK] = pick(flag, out[2], out[1])
        w[rows, 3 * BLOCK:] = out[3]

    groups = (((u, 2), (u, 3)), ((u, 4), (u, 5)), ((u, 1), (u, 6)), ((ur, 0), (ur, 1)))

    def second_cols(g):
        inner = []
        for side, (device, has) in enumerate(sides):
            if g == 3:
                for which in range(2):
                    await_row(u, ur, ux_r, which, side)
            rows = jnp.concatenate([buf[i, :, HALVES[side]] for buf, i in groups[g]], axis=0)
            out = dot3(split(rows), (rcs[side, 0], rcs[side, 1]))
            halves = out[:, :BLOCK], out[:, BLOCK:]
            ts[g, side] = halves[side]
            inner.append(halves[1 - side])
            copy = remote(
                ts.at[g, side], tr.at[g, 1 - side],
                tx_s.at[g, side], tx_r.at[g, 1 - side], device,
            )
            side_copies.append((copy, has))

            @pl.when(has)
            def _():
                copy.start()

        flag = col_flag(1)
        tmid[g, :, :BLOCK] = pick(flag, inner[0], inner[1])
        tmid[g, :, BLOCK:] = pick(flag, inner[1], inner[0])

    def await_sides(g, outer, got, recv):
        for side, (device, has) in enumerate(sides):
            @pl.when(has)
            def _():
                arrived(got.at[g, side], recv.at[g, side])

            @pl.when(jnp.logical_not(has))
            def _():
                got[g, side] = outer[g, side]

    for t in range(2):
        y_begin(t)
    pieces_send()
    halo_send(0)
    across_send()
    y_first(0)
    y_first(1)
    z_begin(0)
    halo_send(3)
    y_second(0)
    z_first(0)
    z_begin(1)
    halo_send(1)
    y_second(1)
    z_first(1)
    y_third(0)
    halo_send(2)
    z_second(0)
    y_third(1)
    load.wait()
    mate_wait(0)
    split_rows(0)
    z_third(0)
    split_first()
    z_second(1)

    for k in (0, 3, 1, 2):
        first_cols(k)
        mix_rows(0, k, w[pl.ds(k * PAIR, PAIR), :], v)
        if k in (0, 3):
            for half in range(2):
                send_row(v, vr, vx_s, vx_r, k // 3, half)
    mate_wait(1)
    split_rows(1)
    second_rows(1)
    second_rows(2)
    for half in range(2):
        for which, k in ((0, 0), (1, 3)):
            await_row(v, vr, vx_r, which, half)
            second_rows(k, HALVES[half])
            send_row(u, ur, ux_s, ux_r, which, half)
    z_third(1)
    split_second()
    for g in range(4):
        second_cols(g)

    places = {1: (2, 0), 2: (0, 0), 3: (0, 1), 4: (1, 0), 5: (1, 1), 6: (2, 1), 0: (3, 0), 7: (3, 1)}
    finals = [row_flag(1, 0), row_flag(1, 1)]

    def parts(block):
        g, half = places[block]
        rows = pl.ds(half * BLOCK, BLOCK)
        return tr[g, 0, rows], tmid[g, rows], tr[g, 1, rows]

    outs = []

    def emit(position, flag, stay, other=None):
        rows = pl.ds(position * BLOCK, BLOCK)
        values = parts(stay)
        if other is not None:
            values = [pick(flag, a, b) for a, b in zip(values, parts(other))]
        obuf[rows, :BLOCK] = values[0]
        obuf[rows, BLOCK:3 * BLOCK] = values[1]
        obuf[rows, 3 * BLOCK:] = values[2]
        copy = pltpu.make_async_copy(obuf.at[rows], out_ref.at[rows], out_sem.at[position])
        copy.start()
        outs.append(copy)

    await_sides(0, ts, tr, tx_r)
    emit(4, None, 3)
    await_sides(1, ts, tr, tx_r)
    emit(3, None, 4)
    await_sides(2, ts, tr, tx_r)
    emit(1, finals[0], 1, 2)
    emit(2, finals[0], 2, 1)
    emit(5, finals[1], 5, 6)
    emit(6, finals[1], 6, 5)
    await_sides(3, ts, tr, tx_r)
    emit(0, None, 0)
    emit(7, None, 7)

    for copy in started:
        copy.wait_send()
    for h in range(2):
        there, here = across_copy(h)

        @pl.when(jnp.logical_not(stays[h]))
        def _():
            there.wait_send()

    for copy, has in row_copies + side_copies + piece_copies:
        @pl.when(has)
        def _():
            copy.wait_send()

    for copy in outs:
        copy.wait()


def body(covariance, rotations, pairing):
    dma = pltpu.SemaphoreType.DMA
    tile = covariance.shape
    wide = (BLOCK, tile[1])
    outer = pltpu.VMEM((4, 2, PAIR, BLOCK), F32)
    middle = pltpu.VMEM((4, PAIR, PAIR), F32)
    scratch = [
        pltpu.VMEM(tile, F32),
        pltpu.VMEM((2, tile[0], PAIR), F32),
        pltpu.VMEM((2, RP, Y, XH, CORE, 8, PAIR), F32),
        pltpu.VMEM((CB, XL, Z, 2, 8, BLOCK), F32),
        pltpu.VMEM((2, XL, Z, 2, 8, PAIR), F32),
        pltpu.VMEM((2, RP, 2, PAIR, PAIR), B16),
        pltpu.VMEM((CB, 2, PAIR, BLOCK), B16),
        pltpu.VMEM((2, 2, PAIR, PAIR), B16),
        pltpu.VMEM(tile, F32),
        pltpu.VMEM((RB, *wide), F32),
        pltpu.VMEM((2, *wide), F32),
        pltpu.VMEM((RB, *wide), F32),
        pltpu.VMEM((2, *wide), F32),
        outer, outer, middle,
        pltpu.VMEM(tile, F32),
        dma((3,)),
        dma((4, 2)), dma((4, 2)),
        dma((8,)), dma((CB, 2)),
        dma((2,)), dma((2,)),
        dma((2,)), dma((2,)),
        dma((2,)), dma((2,)),
        dma((2, 8)), dma((2, 8)),
        dma((2, 8)), dma((2, 8)),
        dma((2,)), dma((2,)),
        dma((2, 2)), dma((2, 2)),
        dma((2, 2)), dma((2, 2)),
        dma((4, 2)), dma((4, 2)),
        dma((RB,)),
    ]
    return pl.pallas_call(
        kernel,
        out_shape=jax.ShapeDtypeStruct(tile, F32),
        in_specs=[
            pl.BlockSpec(memory_space=pltpu.HBM),
            pl.BlockSpec(memory_space=pltpu.HBM),
            pl.BlockSpec(memory_space=pltpu.SMEM),
        ],
        out_specs=pl.BlockSpec(memory_space=pl.ANY),
        scratch_shapes=scratch,
        compiler_params=pltpu.CompilerParams(
            collective_id=0, has_side_effects=True, vmem_limit_bytes=60 * 2**20
        ),
        cost_estimate=pl.CostEstimate(
            flops=2 * 4 * tile[0] * tile[1] * PAIR, bytes_accessed=8 * tile[0] * tile[1],
            transcendentals=0,
        ),
    )(covariance, rotations, pairing)


def solution(mesh):
    in_specs = (P("row", "col"), P(None, "row", "col", None), P())
    out_specs = P("row", "col")
    return jax.shard_map(body, mesh=mesh, in_specs=in_specs, out_specs=out_specs, check_vma=False)
```

time: 87.5 us -> 77.1 us (0.88)
  the two profiles are of different devices: /device:TPU:1 before, /device:TPU:17 now
where the time goes in v3:
time: 77.1 us; the launch traced here: 76.9 us
  Pallas kernels  73.8 us (96%)
  local copies, waits for them, and re-layouts  3.08 us (4%)
    pallas_call x1, Pallas kernels, body(): pl.pallas_call(kernel, out_shape=jax.ShapeDtypeStruct(tile, F32), in_spec...  73.8 us
    unnamed x1, local copies, waits for them, and re-layouts  3.08 us

profile of v3, /device:TPU:17, one launch (start us, length us, event | category | flops | bytes accessed | tf_op | source)
XLA Modules:
  0.0 76.9 jit_solution(1204230943588425709)
XLA Ops:
  0.0 73.8 %shard_map.37 = f32[1024,512]{1,0:T(8,128)} custom-call(f32[1024,512]{1,0:T(8,128)} %cov_ref.1, f32[2,4,8,256]{3,2,1,0:T(8,128)} %rot_ref.1, s32[2,128]{1,0:T(2,128)} %pair_ref.1), custom_call_target="tpu_custom_call" | custom-call | flops 1073741824 | bytes 4194304 | tf_op jit(solution)/shard_map/pallas_call | solution.py:519
  73.8 3.1 %copy.5 = f32[1024,512]{1,0:T(8,128)} copy(f32[1024,512]{1,0:T(8,128)} %shard_map.37) | data formatting | bytes 4194304

commit v4 on v3

--- a/solution.py
+++ b/solution.py
@@ -396,9 +396,9 @@
     halo_send(1)
     y_second(1)
     z_first(1)
+    z_second(0)
+    halo_send(2)
     y_third(0)
-    halo_send(2)
-    z_second(0)
     y_third(1)
     load.wait()
     mate_wait(0)
@@ -417,15 +417,17 @@
     split_rows(1)
     second_rows(1)
     second_rows(2)
+    z_third(1)
+    split_second()
+    second_cols(0)
+    second_cols(1)
     for half in range(2):
         for which, k in ((0, 0), (1, 3)):
             await_row(v, vr, vx_r, which, half)
             second_rows(k, HALVES[half])
             send_row(u, ur, ux_s, ux_r, which, half)
-    z_third(1)
-    split_second()
-    for g in range(4):
-        second_cols(g)
+    second_cols(2)
+    second_cols(3)
 
     places = {1: (2, 0), 2: (0, 0), 3: (0, 1), 4: (1, 0), 5: (1, 1), 6: (2, 1), 0: (3, 0), 7: (3, 1)}
     finals = [row_flag(1, 0), row_flag(1, 1)]
@@ -478,6 +480,25 @@
 
     for copy in outs:
         copy.wait()
+
+
+def place(src_ref, out_ref, held, load_sem, store_sem):
+    parts = [pl.ds(i * BLOCK, BLOCK) for i in range(RB)]
+    loads = [
+        pltpu.make_async_copy(src_ref.at[rows], held.at[rows], load_sem.at[i])
+        for i, rows in enumerate(parts)
+    ]
+    stores = [
+        pltpu.make_async_copy(held.at[rows], out_ref.at[rows], store_sem.at[i])
+        for i, rows in enumerate(parts)
+    ]
+    for load in loads:
+        load.start()
+    for load, store in zip(loads, stores):
+        load.wait()
+        store.start()
+    for store in stores:
+        store.wait()
 
 
 def body(covariance, rotations, pairing):
@@ -516,7 +537,7 @@
         dma((4, 2)), dma((4, 2)),
         dma((RB,)),
     ]
-    return pl.pallas_call(
+    mixed = pl.pallas_call(
         kernel,
         out_shape=jax.ShapeDtypeStruct(tile, F32),
         in_specs=[
@@ -534,6 +555,16 @@
             transcendentals=0,
         ),
     )(covariance, rotations, pairing)
+    return pl.pallas_call(
+        place,
+        out_shape=jax.ShapeDtypeStruct(tile, F32),
+        in_specs=[pl.BlockSpec(memory_space=pl.ANY)],
+        out_specs=pl.BlockSpec(memory_space=pl.ANY),
+        scratch_shapes=[
+            pltpu.VMEM(tile, F32), pltpu.SemaphoreType.DMA((RB,)), pltpu.SemaphoreType.DMA((RB,))
+        ],
+        compiler_params=pltpu.CompilerParams(vmem_limit_bytes=60 * 2**20),
+    )(mixed)
 
 
 def solution(mesh):

time: 77.1 us -> 76.3 us (0.990)
  local copies, waits for them, and re-layouts: 3.08 us -> 0 us
  Pallas kernels: 73.8 us -> 76.2 us
    unnamed x1 -> x0, local copies, waits for them, and re-layouts: 3.08 us -> none
    pallas_call x0 -> x1, Pallas kernels: none -> 2.39 us  [body(): pl.pallas_call(place, out_shape=jax.ShapeDtypeStruct(tile, F32), in_specs...]
where the time goes in v4:
time: 76.3 us; the launch traced here: 76.2 us
  Pallas kernels  76.2 us (100%)
    pallas_call x1, Pallas kernels, body(): pl.pallas_call(kernel, out_shape=jax.ShapeDtypeStruct(tile, F32), in_spec...  73.8 us
    pallas_call x1, Pallas kernels, body(): pl.pallas_call(place, out_shape=jax.ShapeDtypeStruct(tile, F32), in_specs...  2.39 us

profile of v4, /device:TPU:17, one launch (start us, length us, event | category | flops | bytes accessed | tf_op | source)
XLA Modules:
  0.0 76.2 jit_solution(5525994781937199421)
XLA Ops:
  0.0 73.8 %shard_map.37.src_ref = f32[1024,512]{1,0:T(8,128)} custom-call(f32[1024,512]{1,0:T(8,128)} %cov_ref.1, f32[2,4,8,256]{3,2,1,0:T(8,128)} %rot_ref.1, s32[2,128]{1,0:T(2,128)} %pair_ref.1), custom_call_target="tpu_custom_call" | custom-call | flops 1073741824 | bytes 4194304 | tf_op jit(solution)/shard_map/pallas_call | solution.py:540
  73.8 2.4 %shard_map.38 = f32[1024,512]{1,0:T(8,128)} custom-call(f32[1024,512]{1,0:T(8,128)} %shard_map.37.src_ref), custom_call_target="tpu_custom_call" | custom-call | tf_op jit(solution)/shard_map/pallas_call | solution.py:558

commit v5 on v4

--- a/solution.py
+++ b/solution.py
@@ -11,6 +11,7 @@
 XL, Z, Y, XH, CORE = 2, 8, 8, 2, 2
 RB, CB = 8, 4
 RP = RB // 2
+PARTS = 4
 MESH = pl.DeviceIdType.MESH
 F32, B16 = jnp.float32, jnp.bfloat16
 
@@ -483,7 +484,8 @@
 
 
 def place(src_ref, out_ref, held, load_sem, store_sem):
-    parts = [pl.ds(i * BLOCK, BLOCK) for i in range(RB)]
+    rows_each = src_ref.shape[0] // PARTS
+    parts = [pl.ds(i * rows_each, rows_each) for i in range(PARTS)]
     loads = [
         pltpu.make_async_copy(src_ref.at[rows], held.at[rows], load_sem.at[i])
         for i, rows in enumerate(parts)
@@ -561,7 +563,7 @@
         in_specs=[pl.BlockSpec(memory_space=pl.ANY)],
         out_specs=pl.BlockSpec(memory_space=pl.ANY),
         scratch_shapes=[
-            pltpu.VMEM(tile, F32), pltpu.SemaphoreType.DMA((RB,)), pltpu.SemaphoreType.DMA((RB,))
+            pltpu.VMEM(tile, F32), pltpu.SemaphoreType.DMA((PARTS,)), pltpu.SemaphoreType.DMA((PARTS,))
         ],
         compiler_params=pltpu.CompilerParams(vmem_limit_bytes=60 * 2**20),
     )(mixed)

time: 76.3 us -> 76.4 us (level)
  no operation moved by 1% of the time
where the time goes in v5:
time: 76.4 us; the launch traced here: 76.2 us
  Pallas kernels  76.2 us (100%)
    pallas_call x1, Pallas kernels, body(): pl.pallas_call(kernel, out_shape=jax.ShapeDtypeStruct(tile, F32), in_spec...  73.8 us
    pallas_call x1, Pallas kernels, body(): pl.pallas_call(place, out_shape=jax.ShapeDtypeStruct(tile, F32), in_specs...  2.42 us

profile of v5, /device:TPU:17, one launch (start us, length us, event | category | flops | bytes accessed | tf_op | source)
XLA Modules:
  0.0 76.2 jit_solution(925512709560533171)
XLA Ops:
  0.0 73.8 %shard_map.37.src_ref = f32[1024,512]{1,0:T(8,128)} custom-call(f32[1024,512]{1,0:T(8,128)} %cov_ref.1, f32[2,4,8,256]{3,2,1,0:T(8,128)} %rot_ref.1, s32[2,128]{1,0:T(2,128)} %pair_ref.1), custom_call_target="tpu_custom_call" | custom-call | flops 1073741824 | bytes 4194304 | tf_op jit(solution)/shard_map/pallas_call | solution.py:542
  73.8 2.4 %shard_map.38 = f32[1024,512]{1,0:T(8,128)} custom-call(f32[1024,512]{1,0:T(8,128)} %shard_map.37.src_ref), custom_call_target="tpu_custom_call" | custom-call | tf_op jit(solution)/shard_map/pallas_call | solution.py:560
